TPU v7x, 32 devices: a whole 2x2x4 slice. The times are simulated.
32 devices in a mesh: parts: 1, ctx: 4 (over z), pb: 4 (over y, x), row: 2 (over core).
Axes of the slice: x: 2, y: 2, z: 4, core: 2. Of those that a mesh axis runs over, the one named last changes fastest.
Arguments:
- queries: bfloat16 [2048, 3072], P(('parts', 'ctx', 'pb', 'row')), may hold values from -10 to 10
- cache_keys: bfloat16 [4096, 192], P(('parts', 'ctx')), may hold values from -10 to 10
- cache_values: bfloat16 [4096, 128], P(('parts', 'ctx')), may hold values from -6 to 6
- span_keys: bfloat16 [2048, 192], P(('parts', 'ctx')), may hold values from -10 to 10
- span_values: bfloat16 [2048, 128], P(('parts', 'ctx')), may hold values from -6 to 6
- pool_keys: float32 [32, 192], replicated, may hold values from 0.2 to 0.6
- pool_values: float32 [32, 128], replicated, may hold values from 0.05 to 0.3
- gate_logits: bfloat16 [2048, 48], P(('parts', 'ctx', 'pb', 'row')), may hold values from -6 to 6
- chosen_blocks: int32 [32, 16], P(('parts', 'ctx', 'pb', 'row')), may hold values from 0 to 95, as said below
- valid_counts: int32 [32], P(('parts', 'ctx', 'pb', 'row')), may hold values from 4 to 16
Outputs:
- mixed: bfloat16 [2048, 2048], P(('parts', 'ctx', 'pb', 'row'))
Inputs may be any that keep to these rules, and one draw needn't show every extreme that they name: `chosen_blocks`: slot 0 of tile t holds the tile's own block 64 + t. Slot s > 0 holds a block of the cache stored by ctx index (c + s) mod (4), where c is the ctx index that holds tile t; the blocks of one tile are distinct. Slots at or beyond the tile's valid count hold blocks too and are ignored.
All inputs are finite; a program needn't handle non-finite values.
Results may differ from a plain program's by a relative error of at most 0.0034.
The roundings to bfloat16 on the way count: a program that leaves them out, or rounds other values in their place, can miss the bound.
Values may be sent and summed in bfloat16 or wider, within the bound.
A program may use at most 64 MiB of HBM per device.

v0:
```python
import math
import jax
import jax.numpy as jnp
from jax import lax
from jax.sharding import PartitionSpec as P

HEADS = 16
CLEN = 32
STRIDE = 16
BLOCK = 64
WINDOW = 256
NEG_FILL = -1e30


def from_behind(value, axis, steps):
    count = lax.axis_size(axis)
    pairs = [(source, (source + steps) % count) for source in range(count)]
    return lax.ppermute(value, axis, pairs)


def pool_blocks(rows, extra, weights, stride):
    joined = jnp.concatenate([rows, extra], axis=0).astype(jnp.float32)
    blocks = rows.shape[0] // stride
    grouped = joined.reshape(blocks + 1, stride, rows.shape[1])
    leading = jnp.sum(grouped[:-1] * weights[None, :stride, :], axis=1)
    trailing = jnp.sum(grouped[1:] * weights[None, stride:, :], axis=1)
    return (leading + trailing).astype(jnp.bfloat16)


def attend(query_rows, keys, values, visible, score_scale):
    scores = jnp.dot(query_rows, keys.T, preferred_element_type=jnp.float32) * score_scale
    scores = jnp.where(visible, scores, NEG_FILL)
    highest = jnp.max(scores, axis=1, keepdims=True)
    exponent = jnp.where(visible, jnp.exp(scores - highest), 0.0)
    weights = exponent.astype(jnp.bfloat16)
    numerator = jnp.dot(weights, values, preferred_element_type=jnp.float32)
    return numerator / jnp.sum(exponent, axis=1, keepdims=True)


def local(
    queries,
    cache_keys,
    cache_values,
    span_keys,
    span_values,
    pool_keys,
    pool_values,
    gate_logits,
    chosen_blocks,
    valid_counts,
):
    owners = lax.axis_size("ctx")
    ctx_place = lax.axis_index("ctx")
    tile_place = lax.axis_index("pb") * lax.axis_size("row") + lax.axis_index("row")
    cache_len, key_width = cache_keys.shape
    value_width = cache_values.shape[1]
    span_len = span_keys.shape[0]
    tokens = queries.shape[0]
    tiles_here = chosen_blocks.shape[0]
    score_scale = 1.0 / math.sqrt(key_width)
    context_start = cache_len * owners
    local_start = tile_place * tokens
    first_pos = context_start + ctx_place * span_len + local_start
    row_count = tokens * HEADS
    query_rows = queries.reshape(row_count, key_width)
    row_pos = first_pos + jnp.arange(row_count, dtype=jnp.int32) // HEADS
    leader = ctx_place == 0
    outgoing = (
        jnp.where(leader, span_keys[:STRIDE], cache_keys[:STRIDE]),
        jnp.where(leader, span_values[:STRIDE], cache_values[:STRIDE]),
        span_keys[:STRIDE],
        span_values[:STRIDE],
    )
    heads_next = from_behind((outgoing[0], outgoing[1], outgoing[2], outgoing[3]), "ctx", -1)
    summary_keys = jnp.concatenate(
        [
            pool_blocks(cache_keys, heads_next[0], pool_keys, STRIDE),
            pool_blocks(span_keys, heads_next[2], pool_keys, STRIDE),
        ],
        axis=0,
    )
    summary_values = jnp.concatenate(
        [
            pool_blocks(cache_values, heads_next[1], pool_values, STRIDE),
            pool_blocks(span_values, heads_next[3], pool_values, STRIDE),
        ],
        axis=0,
    )
    cache_blocks = cache_len // STRIDE
    span_blocks = span_len // STRIDE
    per_ctx = cache_blocks + span_blocks
    first_row = jnp.int32(0)
    running_max = jnp.full((row_count,), NEG_FILL, jnp.float32)
    running_sum = jnp.zeros((row_count,), jnp.float32)
    running_out = jnp.zeros((row_count, value_width), jnp.float32)
    part_keys = lax.all_gather(summary_keys, "ctx", axis=0, tiled=True)
    part_values = lax.all_gather(summary_values, "ctx", axis=0, tiled=True)
    length = part_keys.shape[0]
    for lower_row in range(0, length, 512):
        upper_row = min(lower_row + 512, length)
        block_index = first_row + lower_row + jnp.arange(upper_row - lower_row, dtype=jnp.int32)
        owner_of = block_index // per_ctx
        within = block_index % per_ctx
        block_id = jnp.where(
            within < cache_blocks,
            owner_of * cache_blocks + within,
            owners * cache_blocks + owner_of * span_blocks + within - cache_blocks,
        )
        visible = (block_id * STRIDE + CLEN)[None, :] <= row_pos[:, None] + 1
        scores = (
            jnp.dot(
                query_rows, part_keys[lower_row:upper_row].T, preferred_element_type=jnp.float32
            )
            * score_scale
        )
        scores = jnp.where(visible, scores, NEG_FILL)
        new_max = jnp.maximum(running_max, jnp.max(scores, axis=1))
        exponent = jnp.where(visible, jnp.exp(scores - new_max[:, None]), 0.0)
        fading = jnp.exp(running_max - new_max)
        running_sum = running_sum * fading + jnp.sum(exponent, axis=1)
        running_out = running_out * fading[:, None] + jnp.dot(
            exponent.astype(jnp.bfloat16),
            part_values[lower_row:upper_row],
            preferred_element_type=jnp.float32,
        )
        running_max = new_max
    summary_out = running_out / running_sum[:, None]
    reach = chosen_blocks.shape[1] // owners
    arranged = chosen_blocks.reshape(tiles_here, reach, owners)
    column_of = (jnp.arange(owners, dtype=jnp.int32) - ctx_place) % owners
    requested = jnp.take(arranged, column_of, axis=2)
    wanted = lax.all_to_all(requested, "ctx", split_axis=2, concat_axis=2, tiled=True)
    cache_count = cache_len // BLOCK
    span_count = span_len // BLOCK
    from_cache = (wanted < owners * cache_count)[..., None, None]
    cache_slot = jnp.clip(wanted - ctx_place * cache_count, 0, cache_count - 1)
    span_slot = jnp.clip(wanted - owners * cache_count - ctx_place * span_count, 0, span_count - 1)
    served_keys = jnp.where(
        from_cache,
        cache_keys.reshape(cache_count, BLOCK, key_width)[cache_slot],
        span_keys.reshape(span_count, BLOCK, key_width)[span_slot],
    )
    served_values = jnp.where(
        from_cache,
        cache_values.reshape(cache_count, BLOCK, value_width)[cache_slot],
        span_values.reshape(span_count, BLOCK, value_width)[span_slot],
    )
    fetched_keys, fetched_values = (
        lax.all_to_all(served_keys, "ctx", split_axis=2, concat_axis=2, tiled=True),
        lax.all_to_all(served_values, "ctx", split_axis=2, concat_axis=2, tiled=True),
    )
    last_ctx = ctx_place == owners - 1
    tail_rows = from_behind(
        (
            jnp.where(last_ctx, cache_keys[-WINDOW:], span_keys[-WINDOW:]),
            jnp.where(last_ctx, cache_values[-WINDOW:], span_values[-WINDOW:]),
        ),
        "ctx",
        1,
    )
    reach_keys = jnp.concatenate([tail_rows[0], span_keys], axis=0)
    reach_values = jnp.concatenate([tail_rows[1], span_values], axis=0)
    gate_values = jax.nn.sigmoid(gate_logits.astype(jnp.float32)).reshape(tokens, 3, HEADS)
    offsets = jnp.arange(BLOCK, dtype=jnp.int32)
    near_offsets = jnp.arange(WINDOW + BLOCK, dtype=jnp.int32)
    slot_number = jnp.arange(reach, dtype=jnp.int32)[:, None] * owners + column_of[None, :]
    key_pos = (requested[0][:, :, None] * BLOCK + offsets).reshape(-1)
    usable = jnp.repeat((slot_number < valid_counts[0]).reshape(-1), BLOCK)
    sel_visible = usable[None, :] & (key_pos[None, :] <= row_pos[:, None])
    picked = attend(
        query_rows,
        fetched_keys[0].reshape(-1, key_width),
        fetched_values[0].reshape(-1, value_width),
        sel_visible,
        score_scale,
    )
    begin = local_start + 0
    near_keys = lax.dynamic_slice_in_dim(reach_keys, begin, WINDOW + BLOCK, 0)
    near_values = lax.dynamic_slice_in_dim(reach_values, begin, WINDOW + BLOCK, 0)
    near_pos = context_start + ctx_place * span_len - WINDOW + begin + near_offsets
    near_visible = (near_pos[None, :] <= row_pos[:, None]) & (
        near_pos[None, :] > row_pos[:, None] - WINDOW
    )
    nearby = attend(query_rows, near_keys, near_values, near_visible, score_scale)
    mixed = (
        gate_values[:, 0, :, None] * summary_out.reshape(BLOCK, HEADS, value_width)
        + gate_values[:, 1, :, None] * picked.reshape(BLOCK, HEADS, value_width)
        + gate_values[:, 2, :, None] * nearby.reshape(BLOCK, HEADS, value_width)
    )
    outputs = mixed.reshape(BLOCK, HEADS * value_width).astype(jnp.bfloat16)
    return outputs


def solution(mesh):
    return jax.shard_map(
        local,
        mesh=mesh,
        in_specs=(
            P(("parts", "ctx", "pb", "row"), None),
            P(("parts", "ctx"), None),
            P(("parts", "ctx"), None),
            P(("parts", "ctx"), None),
            P(("parts", "ctx"), None),
            P(),
            P(),
            P(("parts", "ctx", "pb", "row"), None),
            P(("parts", "ctx", "pb", "row"), None),
            P(("parts", "ctx", "pb", "row")),
        ),
        out_specs=P(("parts", "ctx", "pb", "row"), None),
        check_vma=False,
    )
```

profile of v0, /device:TPU:0, one launch (start us, length us, event | category | flops | bytes accessed | tf_op | source)
XLA Modules:
  0.0 91.8 jit_solution(5316688061465802636)
XLA Ops:
  0.0 1.3 %copy.79 = bf16[1024,192]{1,0:T(8,128)(2,1)S(1)} copy(bf16[1024,192]{0,1:T(8,128)(2,1)} %param.11) | data formatting | bytes 786432 | tf_op args[1]
  1.3 1.1 %copy.77 = bf16[512,192]{1,0:T(8,128)(2,1)S(1)} copy(bf16[512,192]{0,1:T(8,128)(2,1)} %param.13) | data formatting | bytes 393216 | tf_op args[3]
  3.0 5.1 %collective-permute-start = (bf16[16,192]{1,0:T(8,128)(2,1)}, bf16[16,192]{1,0:T(8,128)(2,1)}, u32[]{:S(2)}, u32[]{:S(2)}) collective-permute-start(bf16[16,192]{1,0:T(8,128)(2,1)} %get-tuple-element.13), channel_id=1, source_target_pairs={{0,24},{8,0},{16,8},{24,16},{1,25},{9,1},{17,9},{25,17},{2,26},{10... | collective-permute-start | bytes 18440 | tf_op jit(solution)/shard_map/ppermute | solution.py:18
  8.5 1.3 %slice_select_fusion.3 = (bf16[16,128]{1,0:T(8,128)(2,1)}, bf16[16,128]{1,0:T(8,128)(2,1)}) fusion(bf16[1024,128]{1,0:T(8,128)(2,1)} %param.12, pred[]{:T(512)S(6)} %eq.10, bf16[512,128]{1,0:T(8,128)(2,1)} %param.14), kind=kLoop, calls=%fused_computation.87 | loop fusion | flops 2048 | bytes 16385 | tf_op jit(solution)/shard_map/jit(_where)/select_n | solution.py:70
  10.8 1.3 %reduce.3 = s32[16]{0:T(128)S(1)} reduce(s32[1,16]{1,0:T(1,128)} %param.18, s32[]{:T(128)} %broadcast.494), dimensions={0}, to_apply=%param.18.reduce_sub_computation.3 | reduce | bytes 132 | tf_op args[8]
  13.7 5.3 %all-to-all-start = ((s32[1,4,4]{1,0,2:T(1,128)}), s32[1,4,4]{1,0,2:T(1,128)S(1)}, u32[]{:S(2)}, u32[]{:S(2)}) async-start(s32[1,4,4]{1,0,2:T(1,128)} %copy.85), calls=%async_computation | async-start | bytes 4096 | tf_op jit(solution)/shard_map/all_to_all | solution.py:132
  18.9 1.0 %slice_select_fusion = bf16[256,192]{0,1:T(8,128)(2,1)S(1)} fusion(bf16[512,192]{0,1:T(8,128)(2,1)} %param.13, bf16[1024,192]{0,1:T(8,128)(2,1)} %param.11, pred[]{:T(512)S(6)} %eq.11), kind=kLoop, calls=%fused_computation.60 | loop fusion | flops 49152 | bytes 294913 | tf_op jit(solution)/shard_map/jit(_where)/select_n | solution.py:155
  19.9 2.1 %collective-permute-start.4 = (bf16[256,192]{0,1:T(8,128)(2,1)S(1)}, bf16[256,192]{0,1:T(8,128)(2,1)}, u32[]{:S(2)}, u32[]{:S(2)}) collective-permute-start(bf16[256,192]{0,1:T(8,128)(2,1)S(1)} %slice_select_fusion), channel_id=1, source_target_pairs={{0,8},{8,16},{16,24},{24,0},{1,9},{9,17},{17,25},{25,1},{2,10},{10... | collective-permute-start | bytes 294920 | tf_op jit(solution)/shard_map/ppermute | solution.py:18
  30.3 0.7 copy.95
  31.1 3.6 %all-to-all-start.2 = ((bf16[1,4,4,64,128]{4,3,1,0,2:T(8,128)(2,1)}), bf16[1,4,4,64,128]{4,3,1,0,2:T(8,128)(2,1)S(1)}, u32[]{:S(2)}, u32[]{:S(2)}) async-start(bf16[1,4,4,64,128]{4,3,1,0,2:T(8,128)(2,1)} %copy.95), calls=%async_computation.2 | async-start | bytes 524288 | tf_op jit(solution)/shard_map/all_to_all | solution.py:150
  34.7 0.9 copy_select_fusion
  35.6 2.0 %collective-permute-start.5 = (bf16[256,128]{1,0:T(8,128)(2,1)S(1)}, bf16[256,128]{1,0:T(8,128)(2,1)}, u32[]{:S(2)}, u32[]{:S(2)}) collective-permute-start(bf16[256,128]{1,0:T(8,128)(2,1)S(1)} %slice_select_fusion.1), channel_id=1, source_target_pairs={{0,8},{8,16},{16,24},{24,0},{1,9},{9,17},{17,25},{25,1},{2,10},{10... | collective-permute-start | bytes 196616 | tf_op jit(solution)/shard_map/ppermute | solution.py:18
  39.6 13.2 %all_gather.7 = bf16[384,128]{1,0:T(8,128)(2,1)S(1)} all-gather(bf16[96,128]{1,0:T(8,128)(2,1)S(1)} %pad_maximum_fusion.1), channel_id=1, replica_groups=mesh['parts'=1,'ctx'=4,'pb'=4,'row'=2] {'ctx'}, dimensions={0}, use_global_device_ids=true | all-gather | bytes 122880 | tf_op jit(solution)/shard_map/all_gather | solution.py:97
  52.8 0.8 maximum_convert_fusion
  53.8 0.7 maximum_convert_fusion.1
  55.5 13.6 %all_gather.6 = bf16[384,192]{1,0:T(8,128)(2,1)S(1)} all-gather(bf16[96,192]{1,0:T(8,128)(2,1)S(1)} %pad_maximum_fusion), channel_id=1, replica_groups=mesh['parts'=1,'ctx'=4,'pb'=4,'row'=2] {'ctx'}, dimensions={0}, use_global_device_ids=true | all-gather | bytes 184320 | tf_op jit(solution)/shard_map/all_gather | solution.py:96
  70.6 3.7 %all-to-all-start.1 = ((bf16[1,4,4,64,192]{4,3,1,0,2:T(8,128)(2,1)}), bf16[1,4,4,64,192]{4,3,1,0,2:T(8,128)(2,1)S(1)}, u32[]{:S(2)}, u32[]{:S(2)}) async-start(bf16[1,4,4,64,192]{4,3,1,0,2:T(8,128)(2,1)} %copy_select_fusion), calls=%async_computation.1 | async-start | bytes 1048576 | tf_op jit(solution)/shard_map/all_to_all | solution.py:149
  74.3 1.7 %fusion.59 = (f32[1024]{0:T(1024)S(1)}, f32[1024,320]{0,1:T(8,128)S(1)}) fusion(bf16[1024,192]{1,0:T(8,128)(2,1)S(1)} %reshape.297, s32[]{:T(128)S(6)} %select_n.211, bf16[256,192]{0,1:T(8,128)(2,1)} %collective-permute-done.4, bf16[512,192]{0,1:T(8,128)(2,1)S(1)} %copy-done.2, s32[1024]{0:T(1024)S(1)} %broadcast_add_fusion, s32[1024]{0:T(1024)S(1)} %fusion.31, ...), kind=kOutput, calls=%fused_computation.137 | convolution fusion | flops 128039936 | bytes 2012420 | tf_op jit(solution)/shard_map/dot_general | solution.py:31
  76.4 1.5 %convolution_divide_fusion = f32[1024,128]{1,0:T(8,128)S(1)} fusion(f32[1024,320]{0,1:T(8,128)S(1)} %get-tuple-element.29, f32[1024]{0:T(1024)S(1)} %get-tuple-element.28, s32[1024]{0:T(1024)S(1)} %broadcast_add_fusion, s32[1024]{0:T(1024)S(1)} %fusion.31, s32[320]{0:T(512)S(1)} %iota_add_fusion.1, f32[1024]{0:T(1024)S(1)} %fusion.11, s32[]{:T(128)S(6)} %select_n.211, ...), kind=kOutput, calls=%fused_computation.21 | convolution fusion | flops 86147072 | bytes 2049284 | tf_op jit(solution)/shard_map/dot_general | solution.py:36
  78.0 6.4 %all-to-all-done.1 = bf16[1,4,4,64,192]{4,3,1,0,2:T(8,128)(2,1)S(1)} async-done(((bf16[1,4,4,64,192]{4,3,1,0,2:T(8,128)(2,1)}), bf16[1,4,4,64,192]{4,3,1,0,2:T(8,128)(2,1)S(1)}, u32[]{:S(2)}, u32[]{:S(2)}) %all-to-all-start.1) | async-done | bytes 393248 | tf_op jit(solution)/shard_map/all_to_all | solution.py:149
  84.4 1.2 %fusion = (f32[1024]{0:T(1024)S(1)}, f32[1024,1024]{1,0:T(8,128)S(1)}) fusion(s32[1024]{0:T(1024)S(1)} %fusion.31, s32[1024]{0:T(1024)S(1)} %add.265, pred[1024]{0:T(1024)(128)(4,1)S(1)} %copy-done.11, bf16[1024,192]{1,0:T(8,128)(2,1)S(1)} %bitcast.97, bf16[1024,192]{1,0:T(8,128)(2,1)S(1)} %reshape.297), kind=kOutput, calls=%fused_computation.8 | convolution fusion | flops 407895040 | bytes 4994048 | tf_op jit(solution)/shard_map/dot_general | solution.py:31
  85.6 1.9 %fusion.52 = f32[1024]{0:T(1024)S(1)} fusion(f32[1024]{0:T(1024)S(1)} %get-tuple-element.30, f32[1024,1024]{1,0:T(8,128)S(1)} %get-tuple-element.31, s32[1024]{0:T(1024)S(1)} %fusion.31, s32[1024]{0:T(1024)S(1)} %add.265, pred[1024]{0:T(1024)(128)(4,1)S(1)} %copy-done.11), kind=kLoop, calls=%fused_computation.130 | loop fusion | flops 7339008 | bytes 4211712 | tf_op jit(solution)/shard_map/reduce_sum | solution.py:37
  87.5 1.8 %fusion.6 = f32[1024,128]{1,0:T(8,128)S(1)} fusion(bf16[1024,128]{1,0:T(8,128)(2,1)S(1)} %bitcast.98, f32[1024]{0:T(1024)S(1)} %fusion.52, f32[1024,1024]{1,0:T(8,128)S(1)} %get-tuple-element.31, f32[1024]{0:T(1024)S(1)} %get-tuple-element.30, s32[1024]{0:T(1024)S(1)} %fusion.31, s32[1024]{0:T(1024)S(1)} %add.265, pred[1024]{0:T(1024)(128)(4,1)S(1)} %copy-done.11), kind=kOutput, calls=%fused_computation.20 | convolution fusion | flops 275906560 | bytes 4998144 | tf_op jit(solution)/shard_map/dot_general | solution.py:36
  90.6 1.3 %fusion.25 = bf16[64,2048]{1,0:T(8,128)(2,1)} fusion(f32[64,2048]{1,0:T(8,128)S(1)} %reshape.305, f32[8,8,16,128]{3,2,1,0:T(8,128)S(1)} %bitcast.92, f32[64,2048]{1,0:T(8,128)S(1)} %reshape.304, f32[8,8,16,128]{3,2,1,0:T(8,128)S(1)} %bitcast.91, f32[64,2048]{1,0:T(8,128)S(1)} %reshape.298, f32[8,8,16,128]{3,2,1,0:T(8,128)S(1)} %bitcast.90), kind=kLoop, calls=%fused_computation.40 | loop fusion | flops 786432 | bytes 3407872 | tf_op jit(solution)/shard_map/convert_element_type | solution.py:190
  (115 shorter events, 17.3 us)
Async XLA Ops:
  0.0 22.7 %copy-start.1 = (bf16[1024,128]{1,0:T(8,128)(2,1)S(1)}, bf16[1024,128]{1,0:T(8,128)(2,1)}, u32[]{:S(2)}) copy-start(bf16[1024,128]{1,0:T(8,128)(2,1)} %param.12) | copy-start | bytes 786436
  0.0 22.7 %copy-start = (bf16[512,128]{1,0:T(8,128)(2,1)S(1)}, bf16[512,128]{1,0:T(8,128)(2,1)}, u32[]{:S(2)}) copy-start(bf16[512,128]{1,0:T(8,128)(2,1)} %param.14) | copy-start | bytes 393220
  0.0 22.7 %copy-start.7 = (f32[32,192]{1,0:T(8,128)S(1)}, f32[32,192]{1,0:T(8,128)}, u32[]{:S(2)}) copy-start(f32[32,192]{1,0:T(8,128)} %param.15) | copy-start | bytes 73732
  0.0 22.7 %copy-start.3 = (bf16[64,3072]{1,0:T(8,128)(2,1)S(1)}, bf16[64,3072]{1,0:T(8,128)(2,1)}, u32[]{:S(2)}) copy-start(bf16[64,3072]{1,0:T(8,128)(2,1)} %param.10) | copy-start | bytes 1179652
  0.0 23.4 %copy-start.8 = (f32[32,128]{1,0:T(8,128)S(1)}, f32[32,128]{1,0:T(8,128)}, u32[]{:S(2)}) copy-start(f32[32,128]{1,0:T(8,128)} %param.16) | copy-start | bytes 49156
  0.0 25.2 %copy-start.9 = (bf16[64,48]{0,1:T(8,128)(2,1)S(1)}, bf16[64,48]{0,1:T(8,128)(2,1)}, u32[]{:S(2)}) copy-start(bf16[64,48]{0,1:T(8,128)(2,1)} %param.17) | copy-start | bytes 18436
  3.0 49.8 %collective-permute-start = (bf16[16,192]{1,0:T(8,128)(2,1)}, bf16[16,192]{1,0:T(8,128)(2,1)}, u32[]{:S(2)}, u32[]{:S(2)}) collective-permute-start(bf16[16,192]{1,0:T(8,128)(2,1)} %get-tuple-element.13), channel_id=1, source_target_pairs={{0,24},{8,0},{16,8},{24,16},{1,25},{9,1},{17,9},{25,17},{2,26},{10... | collective-permute-start | bytes 18440 | tf_op jit(solution)/shard_map/ppermute | solution.py:18
  8.0 45.7 %collective-permute-start.1 = (bf16[16,192]{1,0:T(8,128)(2,1)}, bf16[16,192]{1,0:T(8,128)(2,1)}, u32[]{:S(2)}, u32[]{:S(2)}) collective-permute-start(bf16[16,192]{1,0:T(8,128)(2,1)} %get-tuple-element.14), channel_id=1, source_target_pairs={{0,24},{8,0},{16,8},{24,16},{1,25},{9,1},{17,9},{25,17},{2,26},{10... | collective-permute-start | bytes 18440 | tf_op jit(solution)/shard_map/ppermute | solution.py:18
  9.8 25.8 %collective-permute-start.2 = (bf16[16,128]{1,0:T(8,128)(2,1)}, bf16[16,128]{1,0:T(8,128)(2,1)}, u32[]{:S(2)}, u32[]{:S(2)}) collective-permute-start(bf16[16,128]{1,0:T(8,128)(2,1)} %get-tuple-element.15), channel_id=1, source_target_pairs={{0,24},{8,0},{16,8},{24,16},{1,25},{9,1},{17,9},{25,17},{2,26},{10... | collective-permute-start | bytes 12296 | tf_op jit(solution)/shard_map/ppermute | solution.py:18
  10.2 28.2 %collective-permute-start.3 = (bf16[16,128]{1,0:T(8,128)(2,1)}, bf16[16,128]{1,0:T(8,128)(2,1)}, u32[]{:S(2)}, u32[]{:S(2)}) collective-permute-start(bf16[16,128]{1,0:T(8,128)(2,1)} %get-tuple-element.16), channel_id=1, source_target_pairs={{0,24},{8,0},{16,8},{24,16},{1,25},{9,1},{17,9},{25,17},{2,26},{10... | collective-permute-start | bytes 12296 | tf_op jit(solution)/shard_map/ppermute | solution.py:18
  13.7 13.6 %all-to-all-start = ((s32[1,4,4]{1,0,2:T(1,128)}), s32[1,4,4]{1,0,2:T(1,128)S(1)}, u32[]{:S(2)}, u32[]{:S(2)}) async-start(s32[1,4,4]{1,0,2:T(1,128)} %copy.85), calls=%async_computation | async-start | bytes 4096 | tf_op jit(solution)/shard_map/all_to_all | solution.py:132
  19.9 54.4 %collective-permute-start.4 = (bf16[256,192]{0,1:T(8,128)(2,1)S(1)}, bf16[256,192]{0,1:T(8,128)(2,1)}, u32[]{:S(2)}, u32[]{:S(2)}) collective-permute-start(bf16[256,192]{0,1:T(8,128)(2,1)S(1)} %slice_select_fusion), channel_id=1, source_target_pairs={{0,8},{8,16},{16,24},{24,0},{1,9},{9,17},{17,25},{25,1},{2,10},{10... | collective-permute-start | bytes 294920 | tf_op jit(solution)/shard_map/ppermute | solution.py:18
  31.1 39.6 %all-to-all-start.2 = ((bf16[1,4,4,64,128]{4,3,1,0,2:T(8,128)(2,1)}), bf16[1,4,4,64,128]{4,3,1,0,2:T(8,128)(2,1)S(1)}, u32[]{:S(2)}, u32[]{:S(2)}) async-start(bf16[1,4,4,64,128]{4,3,1,0,2:T(8,128)(2,1)} %copy.95), calls=%async_computation.2 | async-start | bytes 524288 | tf_op jit(solution)/shard_map/all_to_all | solution.py:150
  35.6 40.8 %collective-permute-start.5 = (bf16[256,128]{1,0:T(8,128)(2,1)S(1)}, bf16[256,128]{1,0:T(8,128)(2,1)}, u32[]{:S(2)}, u32[]{:S(2)}) collective-permute-start(bf16[256,128]{1,0:T(8,128)(2,1)S(1)} %slice_select_fusion.1), channel_id=1, source_target_pairs={{0,8},{8,16},{16,24},{24,0},{1,9},{9,17},{17,25},{25,1},{2,10},{10... | collective-permute-start | bytes 196616 | tf_op jit(solution)/shard_map/ppermute | solution.py:18
  54.6 14.4 %copy-start.10 = (s32[384]{0:T(512)S(1)}, s32[384]{0:T(512)}, u32[]{:S(2)}) copy-start(s32[384]{0:T(512)} %multiply_add_fusion) | copy-start | bytes 4612
  70.5 3.8 %copy-start.2 = (bf16[512,192]{0,1:T(8,128)(2,1)S(1)}, bf16[512,192]{0,1:T(8,128)(2,1)}, u32[]{:S(2)}) copy-start(bf16[512,192]{0,1:T(8,128)(2,1)} %param.13) | copy-start | bytes 589828
  70.6 13.7 %all-to-all-start.1 = ((bf16[1,4,4,64,192]{4,3,1,0,2:T(8,128)(2,1)}), bf16[1,4,4,64,192]{4,3,1,0,2:T(8,128)(2,1)S(1)}, u32[]{:S(2)}, u32[]{:S(2)}) async-start(bf16[1,4,4,64,192]{4,3,1,0,2:T(8,128)(2,1)} %copy_select_fusion), calls=%async_computation.1 | async-start | bytes 1048576 | tf_op jit(solution)/shard_map/all_to_all | solution.py:149
  77.9 6.5 %copy-start.11 = (pred[1024]{0:T(1024)(128)(4,1)S(1)}, pred[1024]{0:T(1024)(128)(4,1)}, u32[]{:S(2)}) copy-start(pred[1024]{0:T(1024)(128)(4,1)} %and.99) | copy-start | bytes 3076
  87.5 2.0 %copy-start.4 = (f32[64,16]{1,0:T(8,128)S(1)}, f32[64,16]{1,0:T(8,128)}, u32[]{:S(2)}) copy-start(f32[64,16]{1,0:T(8,128)} %copy.76) | copy-start | bytes 12292
  89.4 0.8 copy-start.5
  89.4 0.9 %copy-start.6 = (f32[64,16]{1,0:T(8,128)S(1)}, f32[64,16]{1,0:T(8,128)}, u32[]{:S(2)}) copy-start(f32[64,16]{1,0:T(8,128)} %copy.97) | copy-start | bytes 12292
where the time goes:
time: 92.6 us; the launch traced here: 91.8 us
  blocking collectives  26.8 us (29%)
  starting transfers between devices  22.7 us (25%)
  other arithmetic  14.1 us (15%)
  local copies, waits for them, and re-layouts  13.3 us (14%)
  matrix products  7.31 us (8%)
  waiting for transfers between devices  6.38 us (7%)
  between operations  1.25 us (1%)
    all_gather x1, blocking collectives, local(): part_keys = lax.all_gather(summary_keys, 'ctx', axis=0, tiled=True)  13.6 us
    all_gather x1, blocking collectives, local(): part_values = lax.all_gather(summary_values, 'ctx', axis=0, tiled=True)  13.2 us
    ppermute x6, starting transfers between devices, from_behind(): return lax.ppermute(value, axis, pairs)  10.1 us
    all_to_all x1, waiting for transfers between devices, local(): lax.all_to_all(served_keys, 'ctx', split_axis=2, concat_axis=2, tiled=True)  6.36 us
    all_to_all x1, starting transfers between devices, local(): lax.all_to_all(requested, 'ctx', split_axis=2, concat_axis=2, tiled=True)  5.27 us
    all_to_all x1, starting transfers between devices, local(): lax.all_to_all(served_keys, 'ctx', split_axis=2, concat_axis=2, tiled=True)  3.66 us
    all_to_all x1, starting transfers between devices, local(): lax.all_to_all(served_values, 'ctx', split_axis=2, concat_axis=2, tiled=T...  3.63 us
    unnamed x27, local copies, waits for them, and re-layouts  3.33 us
  transfers between devices with their start and end apart: 9, of which 1 were waited for; matrix products, arithmetic and copies ran while one was open for 27% of the time, Pallas kernels for 0%

commit v1 on v0

--- a/solution.py
+++ b/solution.py
@@ -145,9 +145,26 @@
         cache_values.reshape(cache_count, BLOCK, value_width)[cache_slot],
         span_values.reshape(span_count, BLOCK, value_width)[span_slot],
     )
+
+    def remake_the_skins(xs, comm_axis):
+        t1, low = (lax.psum(1, comm_axis), lax.axis_index(comm_axis))
+        clean = xs.shape[2] // t1
+        right_arr = jnp.roll(xs, -low * clean, 2)
+        r_now = lax.slice_in_dim(right_arr, 0, clean, axis=2)
+        crops = [r_now]
+        for c in range(1, t1):
+            block_last = lax.slice_in_dim(right_arr, c * clean, (c + 1) * clean, axis=2)
+            crops.append(
+                lax.ppermute(
+                    block_last, comm_axis, [(src_i, (src_i + c) % t1) for src_i in range(t1)]
+                )
+            )
+        row_out = jnp.concatenate(crops[::-1], 2)
+        return jnp.roll(row_out, (low + 1) * crops[0].shape[2], 2)
+
     fetched_keys, fetched_values = (
         lax.all_to_all(served_keys, "ctx", split_axis=2, concat_axis=2, tiled=True),
-        lax.all_to_all(served_values, "ctx", split_axis=2, concat_axis=2, tiled=True),
+        remake_the_skins(served_values, "ctx"),
     )
     last_ctx = ctx_place == owners - 1
     tail_rows = from_behind(

time: 92.6 us -> 82.4 us (0.89)
  waiting for transfers between devices: 6.38 us -> 0.08 us
  other arithmetic: 14.1 us -> 10 us
  local copies, waits for them, and re-layouts: 13.3 us -> 10.2 us
  blocking collectives: 26.8 us -> 29.9 us
  starting transfers between devices: 22.7 us -> 24.1 us
  matrix products: 7.31 us -> 6.38 us
    all_to_all x1, waiting for transfers between devices: 6.36 us -> 0.01 us  [local(): lax.all_to_all(served_keys, 'ctx', split_axis=2, concat_axis=2, tiled=True)]
    ppermute x0 -> x3, starting transfers between devices: none -> 5 us  [remake_the_skins(): lax.ppermute(block_last, comm_axis, [(src_i, (src_i + c) % t1) for src_i...]
    all_to_all x1 -> x0, starting transfers between devices: 3.63 us -> none  [local(): lax.all_to_all(served_values, 'ctx', split_axis=2, concat_axis=2, tiled=T...]
    convert_element_type x4, other arithmetic: 2.93 us -> 0.17 us  [pool_blocks(): joined = jnp.concatenate([rows, extra], axis=0).astype(jnp.float32)]
    all_gather x1, blocking collectives: 13.2 us -> 15.8 us  [local(): part_values = lax.all_gather(summary_values, 'ctx', axis=0, tiled=True)]
    unnamed x27 -> x17, local copies, waits for them, and re-layouts: 3.33 us -> 3.31 us
  transfers between devices with their start and end apart: 9 -> 11, of which waited for: 1 -> 1; matrix products, arithmetic and copies ran while one was open for 27% -> 21% of each run, Pallas kernels for 0% -> 0%
where the time goes in v1:
time: 82.4 us; the launch traced here: 82 us
  blocking collectives  29.9 us (36%)
  starting transfers between devices  24.1 us (29%)
  local copies, waits for them, and re-layouts  10.2 us (12%)
  other arithmetic  10 us (12%)
  matrix products  6.38 us (8%)
  between operations  1.25 us (2%)
    all_gather x1, blocking collectives, local(): part_values = lax.all_gather(summary_values, 'ctx', axis=0, tiled=True)  15.8 us
    all_gather x1, blocking collectives, local(): part_keys = lax.all_gather(summary_keys, 'ctx', axis=0, tiled=True)  14.1 us
    ppermute x6, starting transfers between devices, from_behind(): return lax.ppermute(value, axis, pairs)  10.2 us
    all_to_all x1, starting transfers between devices, local(): lax.all_to_all(requested, 'ctx', split_axis=2, concat_axis=2, tiled=True)  5.25 us
    ppermute x3, starting transfers between devices, remake_the_skins(): lax.ppermute(block_last, comm_axis, [(src_i, (src_i + c) % t1) for src_i...  5 us
    all_to_all x1, starting transfers between devices, local(): lax.all_to_all(served_keys, 'ctx', split_axis=2, concat_axis=2, tiled=True)  3.59 us
    dot_general x2, matrix products, attend(): numerator = jnp.dot(weights, values, preferred_element_type=jnp.float32)  3.33 us
    unnamed x17, local copies, waits for them, and re-layouts  3.31 us
  transfers between devices with their start and end apart: 11, of which 1 were waited for; matrix products, arithmetic and copies ran while one was open for 21% of the time, Pallas kernels for 0%

profile of v1, /device:TPU:0, one launch (start us, length us, event | category | flops | bytes accessed | tf_op | source)
XLA Modules:
  0.0 82.0 jit_solution(17214253620957174573)
XLA Ops:
  0.0 1.3 %copy.56 = bf16[1024,192]{1,0:T(8,128)(2,1)S(1)} copy(bf16[1024,192]{0,1:T(8,128)(2,1)} %param.13) | data formatting | bytes 786432 | tf_op args[1]
  1.3 1.1 %copy.54 = bf16[512,192]{1,0:T(8,128)(2,1)S(1)} copy(bf16[512,192]{0,1:T(8,128)(2,1)} %param.15) | data formatting | bytes 393216 | tf_op args[3]
  2.4 5.1 %collective-permute-start = (bf16[16,192]{1,0:T(8,128)(2,1)S(1)}, bf16[16,192]{1,0:T(8,128)(2,1)S(1)}, u32[]{:S(2)}, u32[]{:S(2)}) collective-permute-start(bf16[16,192]{1,0:T(8,128)(2,1)S(1)} %get-tuple-element.14), channel_id=1, source_target_pairs={{0,24},{8,0},{16,8},{24,16},{1,25},{9,1},{17,9},{25,17},{2,26},{10... | collective-permute-start | bytes 18440 | tf_op jit(solution)/shard_map/ppermute | solution.py:18
  8.0 0.7 slice_select_fusion.3
  9.7 1.3 %reduce.3 = s32[16]{0:T(128)S(1)} reduce(s32[1,16]{1,0:T(1,128)} %param.20, s32[]{:T(128)} %broadcast.495), dimensions={0}, to_apply=%param.20.reduce_sub_computation.3 | reduce | bytes 132 | tf_op args[8]
  11.9 0.7 copy.62
  12.6 5.3 %all-to-all-start = ((s32[1,4,4]{1,0,2:T(1,128)}), s32[1,4,4]{1,0,2:T(1,128)S(1)}, u32[]{:S(2)}, u32[]{:S(2)}) async-start(s32[1,4,4]{1,0,2:T(1,128)} %copy.62), calls=%async_computation | async-start | bytes 4096 | tf_op jit(solution)/shard_map/all_to_all | solution.py:132
  17.8 1.0 %slice_select_fusion = bf16[256,192]{0,1:T(8,128)(2,1)S(1)} fusion(bf16[512,192]{0,1:T(8,128)(2,1)} %param.15, bf16[1024,192]{0,1:T(8,128)(2,1)} %param.13, pred[]{:T(512)S(6)} %eq.13), kind=kLoop, calls=%fused_computation.78 | loop fusion | flops 49152 | bytes 294913 | tf_op jit(solution)/shard_map/jit(_where)/select_n | solution.py:172
  18.8 2.1 %collective-permute-start.7 = (bf16[256,192]{0,1:T(8,128)(2,1)S(1)}, bf16[256,192]{0,1:T(8,128)(2,1)S(1)}, u32[]{:S(2)}, u32[]{:S(2)}) collective-permute-start(bf16[256,192]{0,1:T(8,128)(2,1)S(1)} %slice_select_fusion), channel_id=1, source_target_pairs={{0,8},{8,16},{16,24},{24,0},{1,9},{9,17},{17,25},{25,1},{2,10},{10... | collective-permute-start | bytes 294920 | tf_op jit(solution)/shard_map/ppermute | solution.py:18
  25.1 0.9 %copy_select_fusion = bf16[1,4,4,64,192]{4,3,1,0,2:T(8,128)(2,1)} fusion(bf16[1,4,4,64,192]{4,3,2,1,0:T(8,128)(2,1)S(1)} %bitcast.89, bf16[1,4,4,64,192]{4,3,2,1,0:T(8,128)(2,1)S(1)} %bitcast.88, pred[4,4]{0,1:T(4,128)(4,1)S(1)} %copy.64), kind=kLoop, calls=%fused_computation.54 | loop fusion | flops 196608 | bytes 1179664 | tf_op jit(solution)/shard_map/jit(_where)/select_n | solution.py:138
  26.0 3.6 %all-to-all-start.1 = ((bf16[1,4,4,64,192]{4,3,1,0,2:T(8,128)(2,1)}), bf16[1,4,4,64,192]{4,3,1,0,2:T(8,128)(2,1)S(1)}, u32[]{:S(2)}, u32[]{:S(2)}) async-start(bf16[1,4,4,64,192]{4,3,1,0,2:T(8,128)(2,1)} %copy_select_fusion), calls=%async_computation.1 | async-start | bytes 1048576 | tf_op jit(solution)/shard_map/all_to_all | solution.py:166
  31.0 2.1 %collective-permute-start.8 = (bf16[256,128]{1,0:T(8,128)(2,1)S(1)}, bf16[256,128]{1,0:T(8,128)(2,1)}, u32[]{:S(2)}, u32[]{:S(2)}) collective-permute-start(bf16[256,128]{1,0:T(8,128)(2,1)S(1)} %slice_select_fusion.1), channel_id=1, source_target_pairs={{0,8},{8,16},{16,24},{24,0},{1,9},{9,17},{17,25},{25,1},{2,10},{10... | collective-permute-start | bytes 196616 | tf_op jit(solution)/shard_map/ppermute | solution.py:18
  33.2 1.9 %collective-permute-start.4 = (bf16[1,4,1,64,128]{4,3,2,1,0:T(8,128)(2,1)S(1)}, bf16[1,4,1,64,128]{4,3,2,1,0:T(8,128)(2,1)S(1)}, u32[]{:S(2)}, u32[]{:S(2)}) collective-permute-start(bf16[1,4,1,64,128]{4,3,2,1,0:T(8,128)(2,1)S(1)} %get-tuple-element.19), channel_id=1, source_target_pairs={{0,24},{8,0},{16,8},{24,16},{1,25},{9,1},{17,9},{25,17},{2,26},{10... | collective-permute-start | bytes 196616 | tf_op jit(solution)/shard_map/ppermute | solution.py:158
  35.6 15.8 %all_gather.7 = bf16[384,128]{1,0:T(8,128)(2,1)S(1)} all-gather(bf16[96,128]{1,0:T(8,128)(2,1)S(1)} %pad_maximum_fusion.1), channel_id=1, replica_groups=mesh['parts'=1,'ctx'=4,'pb'=4,'row'=2] {'ctx'}, dimensions={0}, use_global_device_ids=true | all-gather | bytes 122880 | tf_op jit(solution)/shard_map/all_gather | solution.py:97
  51.4 0.6 collective-permute-start.5
  52.3 2.5 %collective-permute-start.6 = (bf16[1,4,1,64,128]{4,3,2,1,0:T(8,128)(2,1)S(1)}, bf16[1,4,1,64,128]{4,3,2,1,0:T(8,128)(2,1)S(1)}, u32[]{:S(2)}, u32[]{:S(2)}) collective-permute-start(bf16[1,4,1,64,128]{4,3,2,1,0:T(8,128)(2,1)S(1)} %get-tuple-element.17), channel_id=1, source_target_pairs={{0,8},{8,16},{16,24},{24,0},{1,9},{9,17},{17,25},{25,1},{2,10},{10... | collective-permute-start | bytes 196616 | tf_op jit(solution)/shard_map/ppermute | solution.py:158
  55.7 14.1 %all_gather.6 = bf16[384,192]{1,0:T(8,128)(2,1)S(1)} all-gather(bf16[96,192]{1,0:T(8,128)(2,1)S(1)} %pad_maximum_fusion), channel_id=1, replica_groups=mesh['parts'=1,'ctx'=4,'pb'=4,'row'=2] {'ctx'}, dimensions={0}, use_global_device_ids=true | all-gather | bytes 184320 | tf_op jit(solution)/shard_map/all_gather | solution.py:96
  70.7 0.7 fusion.5
  72.3 0.7 fusion.68
  73.4 1.5 %convolution_divide_fusion = f32[1024,128]{1,0:T(8,128)S(1)} fusion(f32[1024,320]{0,1:T(8,128)S(1)} %get-tuple-element.34, f32[1024]{0:T(1024)S(1)} %get-tuple-element.33, s32[1024]{0:T(1024)S(1)} %broadcast_add_fusion, s32[1024]{0:T(1024)S(1)} %fusion.39, s32[320]{0:T(512)S(1)} %iota_add_fusion.1, f32[1024]{0:T(1024)S(1)} %fusion.11, s32[]{:T(128)S(6)} %select_n.220, ...), kind=kOutput, calls=%fused_computation.21 | convolution fusion | flops 86147072 | bytes 2049284 | tf_op jit(solution)/shard_map/dot_general | solution.py:36
  75.1 1.2 %fusion = (f32[1024]{0:T(1024)S(1)}, f32[1024,1024]{1,0:T(8,128)S(1)}) fusion(s32[1024]{0:T(1024)S(1)} %fusion.39, s32[1024]{0:T(1024)S(1)} %add.276, pred[1024]{0:T(1024)(128)(4,1)S(1)} %and.104, bf16[1024,192]{1,0:T(8,128)(2,1)S(1)} %bitcast.97, bf16[1024,192]{1,0:T(8,128)(2,1)S(1)} %reshape.297), kind=kOutput, calls=%fused_computation.8 | convolution fusion | flops 407895040 | bytes 4994048 | tf_op jit(solution)/shard_map/dot_general | solution.py:31
  76.3 1.9 %fusion.60 = f32[1024]{0:T(1024)S(1)} fusion(f32[1024]{0:T(1024)S(1)} %get-tuple-element.35, f32[1024,1024]{1,0:T(8,128)S(1)} %get-tuple-element.36, s32[1024]{0:T(1024)S(1)} %fusion.39, s32[1024]{0:T(1024)S(1)} %add.276, pred[1024]{0:T(1024)(128)(4,1)S(1)} %and.104), kind=kLoop, calls=%fused_computation.148 | loop fusion | flops 7339008 | bytes 4211712 | tf_op jit(solution)/shard_map/reduce_sum | solution.py:37
  78.2 1.8 %fusion.6 = f32[1024,128]{1,0:T(8,128)S(1)} fusion(bf16[1024,128]{1,0:T(8,128)(2,1)S(1)} %bitcast.98, f32[1024]{0:T(1024)S(1)} %fusion.60, f32[1024,1024]{1,0:T(8,128)S(1)} %get-tuple-element.36, f32[1024]{0:T(1024)S(1)} %get-tuple-element.35, s32[1024]{0:T(1024)S(1)} %fusion.39, s32[1024]{0:T(1024)S(1)} %add.276, pred[1024]{0:T(1024)(128)(4,1)S(1)} %and.104), kind=kOutput, calls=%fused_computation.20 | convolution fusion | flops 275906560 | bytes 4998144 | tf_op jit(solution)/shard_map/dot_general | solution.py:36
  80.7 1.3 %fusion.25 = bf16[64,2048]{1,0:T(8,128)(2,1)} fusion(f32[64,2048]{1,0:T(8,128)S(1)} %reshape.305, f32[8,8,16,128]{3,2,1,0:T(8,128)S(1)} %bitcast.92, f32[64,2048]{1,0:T(8,128)S(1)} %reshape.304, f32[8,8,16,128]{3,2,1,0:T(8,128)S(1)} %bitcast.91, f32[64,2048]{1,0:T(8,128)S(1)} %reshape.298, f32[8,8,16,128]{3,2,1,0:T(8,128)S(1)} %bitcast.90), kind=kLoop, calls=%fused_computation.40 | loop fusion | flops 786432 | bytes 3407872 | tf_op jit(solution)/shard_map/convert_element_type | solution.py:207
  (110 shorter events, 11.7 us)
Async XLA Ops:
  0.0 21.0 %copy-start.1 = (bf16[1024,128]{1,0:T(8,128)(2,1)S(1)}, bf16[1024,128]{1,0:T(8,128)(2,1)}, u32[]{:S(2)}) copy-start(bf16[1024,128]{1,0:T(8,128)(2,1)} %param.14) | copy-start | bytes 786436
  0.0 21.0 %copy-start = (bf16[512,128]{1,0:T(8,128)(2,1)S(1)}, bf16[512,128]{1,0:T(8,128)(2,1)}, u32[]{:S(2)}) copy-start(bf16[512,128]{1,0:T(8,128)(2,1)} %param.16) | copy-start | bytes 393220
  0.0 21.1 %copy-start.4 = (f32[32,192]{1,0:T(8,128)S(1)}, f32[32,192]{1,0:T(8,128)}, u32[]{:S(2)}) copy-start(f32[32,192]{1,0:T(8,128)} %param.17) | copy-start | bytes 73732
  0.0 21.1 %copy-start.3 = (bf16[64,3072]{1,0:T(8,128)(2,1)S(1)}, bf16[64,3072]{1,0:T(8,128)(2,1)}, u32[]{:S(2)}) copy-start(bf16[64,3072]{1,0:T(8,128)(2,1)} %param.12) | copy-start | bytes 1179652
  0.0 21.7 %copy-start.5 = (f32[32,128]{1,0:T(8,128)S(1)}, f32[32,128]{1,0:T(8,128)}, u32[]{:S(2)}) copy-start(f32[32,128]{1,0:T(8,128)} %param.18) | copy-start | bytes 49156
  0.0 22.9 %copy-start.6 = (bf16[64,48]{0,1:T(8,128)(2,1)S(1)}, bf16[64,48]{0,1:T(8,128)(2,1)}, u32[]{:S(2)}) copy-start(bf16[64,48]{0,1:T(8,128)(2,1)} %param.19) | copy-start | bytes 18436
  2.4 49.0 %collective-permute-start = (bf16[16,192]{1,0:T(8,128)(2,1)S(1)}, bf16[16,192]{1,0:T(8,128)(2,1)S(1)}, u32[]{:S(2)}, u32[]{:S(2)}) collective-permute-start(bf16[16,192]{1,0:T(8,128)(2,1)S(1)} %get-tuple-element.14), channel_id=1, source_target_pairs={{0,24},{8,0},{16,8},{24,16},{1,25},{9,1},{17,9},{25,17},{2,26},{10... | collective-permute-start | bytes 18440 | tf_op jit(solution)/shard_map/ppermute | solution.py:18
  7.5 44.7 %collective-permute-start.1 = (bf16[16,192]{1,0:T(8,128)(2,1)S(1)}, bf16[16,192]{1,0:T(8,128)(2,1)S(1)}, u32[]{:S(2)}, u32[]{:S(2)}) collective-permute-start(bf16[16,192]{1,0:T(8,128)(2,1)S(1)} %get-tuple-element.15), channel_id=1, source_target_pairs={{0,24},{8,0},{16,8},{24,16},{1,25},{9,1},{17,9},{25,17},{2,26},{10... | collective-permute-start | bytes 18440 | tf_op jit(solution)/shard_map/ppermute | solution.py:18
  8.7 22.4 %collective-permute-start.2 = (bf16[16,128]{1,0:T(8,128)(2,1)S(1)}, bf16[16,128]{1,0:T(8,128)(2,1)S(1)}, u32[]{:S(2)}, u32[]{:S(2)}) collective-permute-start(bf16[16,128]{1,0:T(8,128)(2,1)S(1)} %get-tuple-element.20), channel_id=1, source_target_pairs={{0,24},{8,0},{16,8},{24,16},{1,25},{9,1},{17,9},{25,17},{2,26},{10... | collective-permute-start | bytes 12296 | tf_op jit(solution)/shard_map/ppermute | solution.py:18
  9.1 24.1 %collective-permute-start.3 = (bf16[16,128]{1,0:T(8,128)(2,1)S(1)}, bf16[16,128]{1,0:T(8,128)(2,1)S(1)}, u32[]{:S(2)}, u32[]{:S(2)}) collective-permute-start(bf16[16,128]{1,0:T(8,128)(2,1)S(1)} %get-tuple-element.21), channel_id=1, source_target_pairs={{0,24},{8,0},{16,8},{24,16},{1,25},{9,1},{17,9},{25,17},{2,26},{10... | collective-permute-start | bytes 12296 | tf_op jit(solution)/shard_map/ppermute | solution.py:18
  12.6 10.7 %all-to-all-start = ((s32[1,4,4]{1,0,2:T(1,128)}), s32[1,4,4]{1,0,2:T(1,128)S(1)}, u32[]{:S(2)}, u32[]{:S(2)}) async-start(s32[1,4,4]{1,0,2:T(1,128)} %copy.62), calls=%async_computation | async-start | bytes 4096 | tf_op jit(solution)/shard_map/all_to_all | solution.py:132
  18.8 53.0 %collective-permute-start.7 = (bf16[256,192]{0,1:T(8,128)(2,1)S(1)}, bf16[256,192]{0,1:T(8,128)(2,1)S(1)}, u32[]{:S(2)}, u32[]{:S(2)}) collective-permute-start(bf16[256,192]{0,1:T(8,128)(2,1)S(1)} %slice_select_fusion), channel_id=1, source_target_pairs={{0,8},{8,16},{16,24},{24,0},{1,9},{9,17},{17,25},{25,1},{2,10},{10... | collective-permute-start | bytes 294920 | tf_op jit(solution)/shard_map/ppermute | solution.py:18
  26.0 49.0 %all-to-all-start.1 = ((bf16[1,4,4,64,192]{4,3,1,0,2:T(8,128)(2,1)}), bf16[1,4,4,64,192]{4,3,1,0,2:T(8,128)(2,1)S(1)}, u32[]{:S(2)}, u32[]{:S(2)}) async-start(bf16[1,4,4,64,192]{4,3,1,0,2:T(8,128)(2,1)} %copy_select_fusion), calls=%async_computation.1 | async-start | bytes 1048576 | tf_op jit(solution)/shard_map/all_to_all | solution.py:166
  31.0 42.4 %collective-permute-start.8 = (bf16[256,128]{1,0:T(8,128)(2,1)S(1)}, bf16[256,128]{1,0:T(8,128)(2,1)}, u32[]{:S(2)}, u32[]{:S(2)}) collective-permute-start(bf16[256,128]{1,0:T(8,128)(2,1)S(1)} %slice_select_fusion.1), channel_id=1, source_target_pairs={{0,8},{8,16},{16,24},{24,0},{1,9},{9,17},{17,25},{25,1},{2,10},{10... | collective-permute-start | bytes 196616 | tf_op jit(solution)/shard_map/ppermute | solution.py:18
  33.2 38.2 %collective-permute-start.4 = (bf16[1,4,1,64,128]{4,3,2,1,0:T(8,128)(2,1)S(1)}, bf16[1,4,1,64,128]{4,3,2,1,0:T(8,128)(2,1)S(1)}, u32[]{:S(2)}, u32[]{:S(2)}) collective-permute-start(bf16[1,4,1,64,128]{4,3,2,1,0:T(8,128)(2,1)S(1)} %get-tuple-element.19), channel_id=1, source_target_pairs={{0,24},{8,0},{16,8},{24,16},{1,25},{9,1},{17,9},{25,17},{2,26},{10... | collective-permute-start | bytes 196616 | tf_op jit(solution)/shard_map/ppermute | solution.py:158
  51.4 20.1 %collective-permute-start.5 = (bf16[1,4,1,64,128]{4,3,2,1,0:T(8,128)(2,1)S(1)}, bf16[1,4,1,64,128]{4,3,2,1,0:T(8,128)(2,1)S(1)}, u32[]{:S(2)}, u32[]{:S(2)}) collective-permute-start(bf16[1,4,1,64,128]{4,3,2,1,0:T(8,128)(2,1)S(1)} %get-tuple-element.18), channel_id=1, source_target_pairs={{0,16},{8,24},{16,0},{24,8},{1,17},{9,25},{17,1},{25,9},{2,18},{10... | collective-permute-start | bytes 196616 | tf_op jit(solution)/shard_map/ppermute | solution.py:158
  52.3 19.2 %collective-permute-start.6 = (bf16[1,4,1,64,128]{4,3,2,1,0:T(8,128)(2,1)S(1)}, bf16[1,4,1,64,128]{4,3,2,1,0:T(8,128)(2,1)S(1)}, u32[]{:S(2)}, u32[]{:S(2)}) collective-permute-start(bf16[1,4,1,64,128]{4,3,2,1,0:T(8,128)(2,1)S(1)} %get-tuple-element.17), channel_id=1, source_target_pairs={{0,8},{8,16},{16,24},{24,0},{1,9},{9,17},{17,25},{25,1},{2,10},{10... | collective-permute-start | bytes 196616 | tf_op jit(solution)/shard_map/ppermute | solution.py:158
  71.3 0.9 %copy-start.2 = (bf16[512,192]{0,1:T(8,128)(2,1)S(1)}, bf16[512,192]{0,1:T(8,128)(2,1)}, u32[]{:S(2)}) copy-start(bf16[512,192]{0,1:T(8,128)(2,1)} %param.15) | copy-start | bytes 589828
